TPU v7x, 32 devices: a whole 2x2x4 slice. The times are simulated.
32 devices in a mesh: parts: 2 (over y), seq: 8 (over z, x), head: 2 (over core).
Axes of the slice: x: 2, y: 2, z: 4, core: 2. Of those that a mesh axis runs over, the one named last changes fastest.
Arguments:
- queries: bfloat16 [4096, 4096], P(('parts', 'seq'), 'head'), parts along dimension 0, may hold values from -144 to 144
- key_rows: bfloat16 [4096, 1024], P(('parts', 'seq'), 'head'), parts along dimension 0, may hold values from -4 to 4
- value_rows: bfloat16 [4096, 1024], P(('parts', 'seq'), 'head'), parts along dimension 0, may hold values from -4 to 4
- out_grad: bfloat16 [4096, 4096], P(('parts', 'seq'), 'head'), parts along dimension 0, may hold values from -4 to 4
- owner_slot: int32 [4096], P(('parts', 'seq')), parts along dimension 0, may hold values from 0 to 2047, as said below
- block_links: int32 [32, 5], P(('parts', 'seq')), parts along dimension 0, may hold values from 0 to 1, as said below
Outputs:
- query_grad: bfloat16 [4096, 4096], P(('parts', 'seq'), 'head'), parts along dimension 0
- key_grad: bfloat16 [4096, 1024], P(('parts', 'seq'), 'head'), parts along dimension 0
- value_grad: bfloat16 [4096, 1024], P(('parts', 'seq'), 'head'), parts along dimension 0
There are 2 independent parts, one for each index of `parts`. A program takes and returns all parts, laid end to end along the dimension named above; each array names one. Nothing has to cross between parts.
Inputs may be any that keep to these rules, and one draw needn't show every extreme that they name: A permutation: token t goes to index owner_slot[t] // 256 of seq, row owner_slot[t] % 256. The 256 tokens of one index of seq send at most 64 tokens to one index, and exactly 64 to some index in every draw. `block_links`: every block is linked to itself (column 2 is 1); columns that name blocks outside the pack are 0.
All inputs are finite; a program needn't handle non-finite values.
Results may differ from a plain program's by a relative error of at most 0.0055.
Values may be sent and summed in bfloat16 or wider, within the bound.
No kernel may reach another device: no remote copies, remote signals or barrier semaphores. Data moves between devices by JAX's collectives and lax.ppermute only.
A program may use at most 64 MiB of HBM per device.

v0:
```python
import jax
import jax.numpy as jnp
from jax import lax
from jax.sharding import PartitionSpec as P

HEAD_DIM = 128
BLOCK = 128


def padded(value, sides, width):
    for axis, dim in sides:
        peers, length = (lax.axis_size(axis), value.shape[dim])
        up = [(i, (i + 1) % peers) for i in range(peers - 1)]
        down = [(j, i) for i, j in up]
        last = lax.slice_in_dim(value, length - width, length, axis=dim)
        leading = lax.slice_in_dim(value, 0, width, axis=dim)
        before = lax.ppermute(last, axis, up)
        after = lax.ppermute(leading, axis, down)
        value = jnp.concatenate([before, value, after], axis=dim)
    return value


def from_behind(value, axis, by):
    peers = lax.axis_size(axis)
    pairs = [(i, i + by) for i in range(peers) if 0 <= i + by < peers]
    return lax.ppermute(value, axis, pairs)


def head_major(matrix, heads):
    return matrix.reshape(matrix.shape[0], heads, -1).transpose(1, 0, 2)


def local(queries, key_rows, value_rows, out_grad, owner_slot, block_links):
    row_count = queries.shape[0]
    seq_count = lax.axis_size("seq")
    capacity = 4 * max(1, row_count // seq_count // 2)
    slots = seq_count * capacity
    kv_width = key_rows.shape[1]
    kv_heads = kv_width // HEAD_DIM
    group_size = queries.shape[1] // kv_width
    score_scale = HEAD_DIM ** (-0.5)
    owner_dev = owner_slot // row_count
    owner_row = owner_slot % row_count
    member = (owner_dev[:, None] == jnp.arange(seq_count, dtype=jnp.int32)[None, :]).astype(
        jnp.int32
    )
    within = jnp.sum(jnp.cumsum(member, 0) * member, 1) - 1
    placed = owner_dev * capacity + within

    def pack_rows(matrix):
        return (
            jnp.zeros((slots, matrix.shape[1]), matrix.dtype)
            .at[placed]
            .set(matrix)
            .reshape(seq_count, capacity, matrix.shape[1])
        )

    vacant = jnp.array([row_count // 16, row_count % 16], jnp.float32)
    row_codes = jnp.stack([owner_row // 16, owner_row % 16], 1).astype(jnp.float32)
    code_buffer = (
        jnp.broadcast_to(vacant, (slots, 2))
        .at[placed]
        .set(row_codes)
        .astype(jnp.bfloat16)
        .reshape(seq_count, capacity, 2)
    )
    q_in, k_in, v_in, g_in, codes_in = (
        lax.all_to_all(pack_rows(queries), "seq", split_axis=0, concat_axis=0, tiled=True),
        lax.all_to_all(pack_rows(key_rows), "seq", split_axis=0, concat_axis=0, tiled=True),
        lax.all_to_all(pack_rows(value_rows), "seq", split_axis=0, concat_axis=0, tiled=True),
        lax.all_to_all(pack_rows(out_grad), "seq", split_axis=0, concat_axis=0, tiled=True),
        lax.all_to_all(code_buffer, "seq", split_axis=0, concat_axis=0, tiled=True),
    )
    arrived = codes_in.reshape(slots, 2).astype(jnp.float32)
    target = (arrived[:, 0] * 16.0 + arrived[:, 1]).astype(jnp.int32)

    def unpack_rows(buffer):
        flat_rows = buffer.reshape(slots, buffer.shape[2])
        return (
            jnp.zeros((row_count, flat_rows.shape[1]), flat_rows.dtype)
            .at[target]
            .set(flat_rows, mode="drop")
        )

    q_own = unpack_rows(q_in)
    k_own = unpack_rows(k_in)
    v_own = unpack_rows(v_in)
    g_own = unpack_rows(g_in)
    blocks = row_count // BLOCK
    span = block_links.shape[1]
    offset = (
        jnp.arange(3 * blocks, dtype=jnp.int32)[None, :]
        - jnp.arange(blocks, dtype=jnp.int32)[:, None]
    )
    selector = offset[:, :, None] == jnp.arange(span, dtype=jnp.int32)[None, None, :]
    allowed = jnp.sum(jnp.where(selector, block_links[:, None, :], 0), 2) > 0
    token_mask = jnp.repeat(jnp.repeat(allowed, BLOCK, 0), BLOCK, 1)
    kv_pair = jnp.concatenate([k_own, v_own], 1)
    kv_wide = padded(kv_pair, (("seq", 0),), row_count)

    def scores_of(q_group, k_group):
        raw_scores = (
            jnp.einsum("rgd,kd->grk", q_group, k_group, preferred_element_type=jnp.float32)
            * score_scale
        )
        return jnp.where(token_mask[None], raw_scores, -jnp.inf)

    def forward_head(operands):
        q_group, k_group, v_group = operands
        scores = scores_of(q_group, k_group)
        row_top = jnp.max(scores, -1, keepdims=True)
        log_total = row_top + jnp.log(jnp.sum(jnp.exp(scores - row_top), -1, keepdims=True))
        probs = jnp.exp(scores - log_total).astype(jnp.bfloat16)
        attended = jnp.einsum(
            "grk,kd->rgd", probs, v_group, preferred_element_type=jnp.float32
        ).astype(jnp.bfloat16)
        return (attended, log_total)

    def backward_head(operands):
        q_group, k_group, v_group, g_group, attended, log_total = operands
        weights = jnp.exp(scores_of(q_group, k_group) - log_total)
        row_delta = jnp.sum(g_group.astype(jnp.float32) * attended.astype(jnp.float32), -1).T[
            :, :, None
        ]
        d_probs = jnp.einsum("rgd,kd->grk", g_group, v_group, preferred_element_type=jnp.float32)
        d_scores = (weights * (d_probs - row_delta)).astype(jnp.bfloat16)
        q_grad = (
            jnp.einsum("grk,kd->rgd", d_scores, k_group, preferred_element_type=jnp.float32)
            * score_scale
        ).astype(jnp.bfloat16)
        k_grad = (
            jnp.einsum("grk,rgd->kd", d_scores, q_group, preferred_element_type=jnp.float32)
            * score_scale
        )
        v_grad = jnp.einsum(
            "grk,rgd->kd", weights.astype(jnp.bfloat16), g_group, preferred_element_type=jnp.float32
        )
        return (q_grad, k_grad, v_grad)

    query_heads = q_own.reshape(row_count, kv_heads, group_size, HEAD_DIM).transpose(1, 0, 2, 3)
    grad_heads = g_own.reshape(row_count, kv_heads, group_size, HEAD_DIM).transpose(1, 0, 2, 3)
    key_heads = head_major(kv_wide[:, :kv_width], kv_heads)
    value_heads = head_major(kv_wide[:, kv_width:], kv_heads)
    attended, log_total = lax.map(forward_head, (query_heads, key_heads, value_heads))
    q_grads, k_grads, v_grads = lax.map(
        backward_head, (query_heads, key_heads, value_heads, grad_heads, attended, log_total)
    )
    q_grad_own = q_grads.transpose(1, 0, 2, 3).reshape(row_count, kv_heads * group_size * HEAD_DIM)
    kv_grads = jnp.concatenate(
        [
            k_grads.transpose(1, 0, 2).reshape(3 * row_count, kv_width),
            v_grads.transpose(1, 0, 2).reshape(3 * row_count, kv_width),
        ],
        1,
    )
    from_above = from_behind(kv_grads[:row_count].astype(jnp.bfloat16), "seq", -1).astype(
        jnp.float32
    )
    from_below = from_behind(kv_grads[2 * row_count :].astype(jnp.bfloat16), "seq", 1).astype(
        jnp.float32
    )
    kv_total = (kv_grads[row_count : 2 * row_count] + from_above + from_below).astype(jnp.bfloat16)
    pick_rows = jnp.minimum(target, row_count - 1)

    def gather_back(matrix):
        return matrix[pick_rows].reshape(seq_count, capacity, matrix.shape[1])

    q_back, k_back, v_back = (
        lax.all_to_all(gather_back(q_grad_own), "seq", split_axis=0, concat_axis=0, tiled=True),
        lax.all_to_all(
            gather_back(kv_total[:, :kv_width]), "seq", split_axis=0, concat_axis=0, tiled=True
        ),
        lax.all_to_all(
            gather_back(kv_total[:, kv_width:]), "seq", split_axis=0, concat_axis=0, tiled=True
        ),
    )

    def settle_rows(buffer):
        return buffer.reshape(slots, buffer.shape[2])[placed]

    return (settle_rows(q_back), settle_rows(k_back), settle_rows(v_back))


def solution(mesh):
    return jax.shard_map(
        local,
        mesh=mesh,
        in_specs=(
            P(("parts", "seq"), "head"),
            P(("parts", "seq"), "head"),
            P(("parts", "seq"), "head"),
            P(("parts", "seq"), "head"),
            P(("parts", "seq")),
            P(("parts", "seq"), None),
        ),
        out_specs=(
            P(("parts", "seq"), "head"),
            P(("parts", "seq"), "head"),
            P(("parts", "seq"), "head"),
        ),
        check_vma=False,
    )
```

profile of v0, /device:TPU:0, one launch (start us, length us, event | category | flops | bytes accessed | tf_op | source)
XLA Modules:
  0.0 340.5 jit_solution(8709919778711682989)
XLA Ops:
  5.2 7.3 %all-to-all-start = ((bf16[8,64,2]{1,2,0:T(2,128)(2,1)}), bf16[8,64,2]{1,2,0:T(2,128)(2,1)S(1)}, u32[]{:S(2)}, u32[]{:S(2)}) async-start(bf16[8,64,2]{1,2,0:T(2,128)(2,1)} %copy.118), calls=%async_computation | async-start | bytes 8192 | tf_op jit(solution)/shard_map/all_to_all | solution.py:72
  12.4 2.7 scatter_custom_fusion.1
  15.1 3.7 %all-to-all-done = bf16[8,64,2]{1,2,0:T(2,128)(2,1)S(1)} async-done(((bf16[8,64,2]{1,2,0:T(2,128)(2,1)}), bf16[8,64,2]{1,2,0:T(2,128)(2,1)S(1)}, u32[]{:S(2)}, u32[]{:S(2)}) %all-to-all-start) | async-done | bytes 2080 | tf_op jit(solution)/shard_map/all_to_all | solution.py:72
  18.8 3.5 %all-to-all-start.1 = ((bf16[8,64,512]{2,1,0:T(8,128)(2,1)}), bf16[8,64,512]{2,1,0:T(8,128)(2,1)S(1)}, u32[]{:S(2)}, u32[]{:S(2)}) async-start(bf16[8,64,512]{2,1,0:T(8,128)(2,1)} %bitcast.7), calls=%async_computation.1 | async-start | bytes 1048576 | tf_op jit(solution)/shard_map/all_to_all | solution.py:69
  22.3 2.7 scatter_custom_fusion.3
  25.0 10.5 %all-to-all-done.1 = bf16[8,64,512]{2,1,0:T(8,128)(2,1)S(1)} async-done(((bf16[8,64,512]{2,1,0:T(8,128)(2,1)}), bf16[8,64,512]{2,1,0:T(8,128)(2,1)S(1)}, u32[]{:S(2)}, u32[]{:S(2)}) %all-to-all-start.1) | async-done | bytes 524320 | tf_op jit(solution)/shard_map/all_to_all | solution.py:69
  35.6 3.7 %all-to-all-start.2 = ((bf16[8,64,512]{2,1,0:T(8,128)(2,1)}), bf16[8,64,512]{2,1,0:T(8,128)(2,1)S(1)}, u32[]{:S(2)}, u32[]{:S(2)}) async-start(bf16[8,64,512]{2,1,0:T(8,128)(2,1)} %bitcast.9), calls=%async_computation.2 | async-start | bytes 1048576 | tf_op jit(solution)/shard_map/all_to_all | solution.py:70
  39.2 4.4 %scatter_custom_fusion.5 = bf16[512,2048]{1,0:T(8,128)(2,1)} fusion(s32[256]{0:T(256)S(1)} %get-tuple-element.326, bf16[256,2048]{1,0:T(8,128)(2,1)} %param.11, bf16[]{:T(256)} %constant.108.clone.1), kind=kCustom, calls=%fused_computation.90 | custom fusion | bytes 2097664 | tf_op jit(solution)/shard_map/scatter | solution.py:54
  43.6 9.5 %all-to-all-done.2 = bf16[8,64,512]{2,1,0:T(8,128)(2,1)S(1)} async-done(((bf16[8,64,512]{2,1,0:T(8,128)(2,1)}), bf16[8,64,512]{2,1,0:T(8,128)(2,1)S(1)}, u32[]{:S(2)}, u32[]{:S(2)}) %all-to-all-start.2) | async-done | bytes 524320 | tf_op jit(solution)/shard_map/all_to_all | solution.py:70
  53.1 4.5 %all-to-all-start.3 = ((bf16[8,64,2048]{2,1,0:T(8,128)(2,1)}), bf16[8,64,2048]{2,1,0:T(8,128)(2,1)}, u32[]{:S(2)}, u32[]{:S(2)}) async-start(bf16[8,64,2048]{2,1,0:T(8,128)(2,1)} %bitcast.13), calls=%async_computation.3 | async-start | bytes 4194304 | tf_op jit(solution)/shard_map/all_to_all | solution.py:68
  57.7 4.4 %scatter_custom_fusion.7 = bf16[512,2048]{1,0:T(8,128)(2,1)} fusion(s32[256]{0:T(256)S(1)} %get-tuple-element.326, bf16[256,2048]{1,0:T(8,128)(2,1)} %param.14, bf16[]{:T(256)} %constant.108.clone.1), kind=kCustom, calls=%fused_computation.88 | custom fusion | bytes 2097664 | tf_op jit(solution)/shard_map/scatter | solution.py:54
  62.2 2.6 scatter_custom_fusion.2
  64.8 2.4 scatter_custom_fusion.4
  67.3 3.8 %collective-permute-start = (bf16[256,1024]{1,0:T(8,128)(2,1)S(1)}, bf16[256,1024]{1,0:T(8,128)(2,1)S(1)}, u32[]{:S(2)}, u32[]{:S(2)}) collective-permute-start(bf16[256,1024]{1,0:T(8,128)(2,1)S(1)} %constant_dynamic-update-slice_fusion), channel_id=1, source_target_pairs={{0,2},{2,4},{4,6},{6,8},{8,10},{10,12},{12,14},{1,3},{3,5},{5,7},{... | collective-permute-start | bytes 1572872 | tf_op jit(solution)/shard_map/ppermute | solution.py:17
  72.6 28.8 %collective-permute-done = bf16[256,1024]{1,0:T(8,128)(2,1)S(1)} collective-permute-done((bf16[256,1024]{1,0:T(8,128)(2,1)S(1)}, bf16[256,1024]{1,0:T(8,128)(2,1)S(1)}, u32[]{:S(2)}, u32[]{:S(2)}) %collective-permute-start) | collective-permute-done | bytes 524320 | tf_op jit(solution)/shard_map/ppermute | solution.py:17
  103.5 3.7 %all-to-all-done.3 = bf16[8,64,2048]{2,1,0:T(8,128)(2,1)} async-done(((bf16[8,64,2048]{2,1,0:T(8,128)(2,1)}), bf16[8,64,2048]{2,1,0:T(8,128)(2,1)}, u32[]{:S(2)}, u32[]{:S(2)}) %all-to-all-start.3) | async-done | bytes 2097184 | tf_op jit(solution)/shard_map/all_to_all | solution.py:68
  107.2 13.3 %all-to-all-start.4 = ((bf16[8,64,2048]{2,1,0:T(8,128)(2,1)}), bf16[8,64,2048]{2,1,0:T(8,128)(2,1)}, u32[]{:S(2)}, u32[]{:S(2)}) async-start(bf16[8,64,2048]{2,1,0:T(8,128)(2,1)} %bitcast.23), calls=%async_computation.4 | async-start | bytes 4194304 | tf_op jit(solution)/shard_map/all_to_all | solution.py:71
  120.5 5.0 %scatter_custom_fusion.6 = bf16[256,2048]{1,0:T(8,128)(2,1)S(1)} fusion(s32[512]{0:T(512)S(1)} %bitcast.259, bf16[512,2048]{1,0:T(8,128)(2,1)} %bitcast.14, bf16[]{:T(256)} %constant.108.clone.1), kind=kCustom, calls=%fused_computation.94 | custom fusion | bytes 1049088 | tf_op jit(solution)/shard_map/scatter | solution.py:82
  126.9 13.4 %while.28 = (s32[]{:T(128)}, bf16[4,256,4,128]{1,3,2,0:T(8,128)(2,1)S(1)}, f32[4,4,256,1]{2,1,3,0:T(4,128)S(1)}, bf16[4,768,128]{1,2,0:T(8,128)(2,1)}, bf16[4,76...) while((s32[]{:T(128)}, ...), condition=%wide.region_16.17_spmd.clone, body=%wide.region_13.16_spmd.clone.sunk | while | flops 411433984 | bytes 11177561 | solution.py:144
  128.3 1.9 fusion.112
  131.7 1.9 fusion.112
  135.0 1.9 fusion.112
  138.3 1.9 fusion.112
  140.3 29.7 %all-to-all-done.4 = bf16[8,64,2048]{2,1,0:T(8,128)(2,1)} async-done(((bf16[8,64,2048]{2,1,0:T(8,128)(2,1)}), bf16[8,64,2048]{2,1,0:T(8,128)(2,1)}, u32[]{:S(2)}, u32[]{:S(2)}) %all-to-all-start.4) | async-done | bytes 2097184 | tf_op jit(solution)/shard_map/all_to_all | solution.py:71
  170.0 5.5 %scatter_custom_fusion.8 = bf16[256,2048]{1,0:T(8,128)(2,1)} fusion(s32[512]{0:T(512)S(1)} %bitcast.260, bf16[512,2048]{1,0:T(8,128)(2,1)} %bitcast.24, bf16[]{:T(256)} %constant.108.clone.1), kind=kCustom, calls=%fused_computation.92 | custom fusion | bytes 1049088 | tf_op jit(solution)/shard_map/scatter | solution.py:82
  175.5 2.3 copy.126
  178.9 39.0 %while.29 = (s32[]{:T(128)}, bf16[4,256,4,128]{1,3,2,0:T(8,128)(2,1)}, f32[4,768,128]{2,1,0:T(8,128)}, f32[4,768,128]{2,1,0:T(8,128)}, bf16[4,768,128]{2,1,0:T(8...) while((s32[]{:T(128)}, ...), condition=%wide.region_19.20_spmd.clone, body=%wide.region_17.19_spmd.clone.sunk | while | flops 1015380992 | bytes 32668368 | solution.py:145
  182.5 2.0 fusion.125
  192.3 2.0 fusion.125
  196.7 1.6 fusion.128
  202.0 2.0 fusion.125
  211.8 2.0 fusion.125
  216.2 1.6 fusion.128
  222.7 4.6 %collective-permute-start.3 = (bf16[256,1024]{1,0:T(8,128)(2,1)S(1)}, bf16[256,1024]{1,0:T(8,128)(2,1)S(1)}, u32[]{:S(2)}, u32[]{:S(2)}) collective-permute-start(bf16[256,1024]{1,0:T(8,128)(2,1)S(1)} %get-tuple-element.320), channel_id=1, source_target_pairs={{0,2},{2,4},{4,6},{6,8},{8,10},{10,12},{12,14},{1,3},{3,5},{5,7},{... | collective-permute-start | bytes 1572872 | tf_op jit(solution)/shard_map/ppermute | solution.py:26
  227.3 9.3 %collective-permute-done.2 = bf16[256,1024]{1,0:T(8,128)(2,1)S(1)} collective-permute-done((bf16[256,1024]{1,0:T(8,128)(2,1)S(1)}, bf16[256,1024]{1,0:T(8,128)(2,1)S(1)}, u32[]{:S(2)}, u32[]{:S(2)}) %collective-permute-start.2) | collective-permute-done | bytes 524320 | tf_op jit(solution)/shard_map/ppermute | solution.py:26
  236.6 9.8 %collective-permute-done.3 = bf16[256,1024]{1,0:T(8,128)(2,1)S(1)} collective-permute-done((bf16[256,1024]{1,0:T(8,128)(2,1)S(1)}, bf16[256,1024]{1,0:T(8,128)(2,1)S(1)}, u32[]{:S(2)}, u32[]{:S(2)}) %collective-permute-start.3) | collective-permute-done | bytes 524320 | tf_op jit(solution)/shard_map/ppermute | solution.py:26
  246.7 2.6 gather_fusion.4
  249.4 4.6 %all-to-all-start.7 = ((bf16[8,64,512]{2,1,0:T(8,128)(2,1)}), bf16[8,64,512]{2,1,0:T(8,128)(2,1)S(1)}, u32[]{:S(2)}, u32[]{:S(2)}) async-start(bf16[8,64,512]{2,1,0:T(8,128)(2,1)} %bitcast.36), calls=%async_computation.7 | async-start | bytes 1048576 | tf_op jit(solution)/shard_map/all_to_all | solution.py:173
  254.0 2.6 gather_fusion.2
  256.6 11.8 %all-to-all-done.7 = bf16[8,64,512]{2,1,0:T(8,128)(2,1)S(1)} async-done(((bf16[8,64,512]{2,1,0:T(8,128)(2,1)}), bf16[8,64,512]{2,1,0:T(8,128)(2,1)S(1)}, u32[]{:S(2)}, u32[]{:S(2)}) %all-to-all-start.7) | async-done | bytes 524320 | tf_op jit(solution)/shard_map/all_to_all | solution.py:173
  268.4 3.6 %all-to-all-start.6 = ((bf16[8,64,512]{2,1,0:T(8,128)(2,1)}), bf16[8,64,512]{2,1,0:T(8,128)(2,1)S(1)}, u32[]{:S(2)}, u32[]{:S(2)}) async-start(bf16[8,64,512]{2,1,0:T(8,128)(2,1)} %bitcast.34), calls=%async_computation.6 | async-start | bytes 1048576 | tf_op jit(solution)/shard_map/all_to_all | solution.py:170
  272.7 3.3 gather_fusion
  276.0 10.3 %all-to-all-done.6 = bf16[8,64,512]{2,1,0:T(8,128)(2,1)S(1)} async-done(((bf16[8,64,512]{2,1,0:T(8,128)(2,1)}), bf16[8,64,512]{2,1,0:T(8,128)(2,1)S(1)}, u32[]{:S(2)}, u32[]{:S(2)}) %all-to-all-start.6) | async-done | bytes 524320 | tf_op jit(solution)/shard_map/all_to_all | solution.py:170
  286.3 3.6 %all-to-all-start.5 = ((bf16[8,64,2048]{2,1,0:T(8,128)(2,1)}), bf16[8,64,2048]{2,1,0:T(8,128)(2,1)S(1)}, u32[]{:S(2)}, u32[]{:S(2)}) async-start(bf16[8,64,2048]{2,1,0:T(8,128)(2,1)} %bitcast.241), calls=%async_computation.5 | async-start | bytes 4194304 | tf_op jit(solution)/shard_map/all_to_all | solution.py:169
  289.9 1.9 gather_fusion.5
  291.8 1.9 gather_fusion.3
  293.6 44.5 %all-to-all-done.5 = bf16[8,64,2048]{2,1,0:T(8,128)(2,1)S(1)} async-done(((bf16[8,64,2048]{2,1,0:T(8,128)(2,1)}), bf16[8,64,2048]{2,1,0:T(8,128)(2,1)S(1)}, u32[]{:S(2)}, u32[]{:S(2)}) %all-to-all-start.5) | async-done | bytes 2097184 | tf_op jit(solution)/shard_map/all_to_all | solution.py:169
  338.2 2.3 gather_fusion.1
  (131 shorter events, 49.6 us)
Async XLA Ops:
  5.2 13.6 %all-to-all-start = ((bf16[8,64,2]{1,2,0:T(2,128)(2,1)}), bf16[8,64,2]{1,2,0:T(2,128)(2,1)S(1)}, u32[]{:S(2)}, u32[]{:S(2)}) async-start(bf16[8,64,2]{1,2,0:T(2,128)(2,1)} %copy.118), calls=%async_computation | async-start | bytes 8192 | tf_op jit(solution)/shard_map/all_to_all | solution.py:72
  18.8 16.8 %all-to-all-start.1 = ((bf16[8,64,512]{2,1,0:T(8,128)(2,1)}), bf16[8,64,512]{2,1,0:T(8,128)(2,1)S(1)}, u32[]{:S(2)}, u32[]{:S(2)}) async-start(bf16[8,64,512]{2,1,0:T(8,128)(2,1)} %bitcast.7), calls=%async_computation.1 | async-start | bytes 1048576 | tf_op jit(solution)/shard_map/all_to_all | solution.py:69
  35.6 17.5 %all-to-all-start.2 = ((bf16[8,64,512]{2,1,0:T(8,128)(2,1)}), bf16[8,64,512]{2,1,0:T(8,128)(2,1)S(1)}, u32[]{:S(2)}, u32[]{:S(2)}) async-start(bf16[8,64,512]{2,1,0:T(8,128)(2,1)} %bitcast.9), calls=%async_computation.2 | async-start | bytes 1048576 | tf_op jit(solution)/shard_map/all_to_all | solution.py:70
  53.1 4.5 %copy-start.4 = (s32[2,5]{1,0:T(2,128)S(1)}, s32[2,5]{1,0:T(2,128)}, u32[]{:S(2)}) copy-start(s32[2,5]{1,0:T(2,128)} %param.16) | copy-start | bytes 124
  53.1 54.1 %all-to-all-start.3 = ((bf16[8,64,2048]{2,1,0:T(8,128)(2,1)}), bf16[8,64,2048]{2,1,0:T(8,128)(2,1)}, u32[]{:S(2)}, u32[]{:S(2)}) async-start(bf16[8,64,2048]{2,1,0:T(8,128)(2,1)} %bitcast.13), calls=%async_computation.3 | async-start | bytes 4194304 | tf_op jit(solution)/shard_map/all_to_all | solution.py:68
  67.3 34.1 %collective-permute-start = (bf16[256,1024]{1,0:T(8,128)(2,1)S(1)}, bf16[256,1024]{1,0:T(8,128)(2,1)S(1)}, u32[]{:S(2)}, u32[]{:S(2)}) collective-permute-start(bf16[256,1024]{1,0:T(8,128)(2,1)S(1)} %constant_dynamic-update-slice_fusion), channel_id=1, source_target_pairs={{0,2},{2,4},{4,6},{6,8},{8,10},{10,12},{12,14},{1,3},{3,5},{5,7},{... | collective-permute-start | bytes 1572872 | tf_op jit(solution)/shard_map/ppermute | solution.py:17
  71.1 30.3 %collective-permute-start.1 = (bf16[256,1024]{1,0:T(8,128)(2,1)S(1)}, bf16[256,1024]{1,0:T(8,128)(2,1)S(1)}, u32[]{:S(2)}, u32[]{:S(2)}) collective-permute-start(bf16[256,1024]{1,0:T(8,128)(2,1)S(1)} %constant_dynamic-update-slice_fusion), channel_id=1, source_target_pairs={{2,0},{4,2},{6,4},{8,6},{10,8},{12,10},{14,12},{3,1},{5,3},{7,5},{... | collective-permute-start | bytes 1572872 | tf_op jit(solution)/shard_map/ppermute | solution.py:18
  107.2 62.8 %all-to-all-start.4 = ((bf16[8,64,2048]{2,1,0:T(8,128)(2,1)}), bf16[8,64,2048]{2,1,0:T(8,128)(2,1)}, u32[]{:S(2)}, u32[]{:S(2)}) async-start(bf16[8,64,2048]{2,1,0:T(8,128)(2,1)} %bitcast.23), calls=%async_computation.4 | async-start | bytes 4194304 | tf_op jit(solution)/shard_map/all_to_all | solution.py:71
  178.9 1.0 copy-start.1
  181.3 1.2 copy-start
  187.0 1.6 copy-start.2
  188.6 1.0 copy-start.1
  191.0 1.2 copy-start
  196.7 1.7 copy-start.2
  198.4 1.0 copy-start.1
  200.8 1.2 copy-start
  206.5 1.6 copy-start.2
  208.1 1.0 copy-start.1
  210.5 1.2 copy-start
  216.2 1.6 copy-start.2
  221.4 15.2 %collective-permute-start.2 = (bf16[256,1024]{1,0:T(8,128)(2,1)S(1)}, bf16[256,1024]{1,0:T(8,128)(2,1)S(1)}, u32[]{:S(2)}, u32[]{:S(2)}) collective-permute-start(bf16[256,1024]{1,0:T(8,128)(2,1)S(1)} %get-tuple-element.319), channel_id=1, source_target_pairs={{2,0},{4,2},{6,4},{8,6},{10,8},{12,10},{14,12},{3,1},{5,3},{7,5},{... | collective-permute-start | bytes 1572872 | tf_op jit(solution)/shard_map/ppermute | solution.py:26
  222.7 23.7 %collective-permute-start.3 = (bf16[256,1024]{1,0:T(8,128)(2,1)S(1)}, bf16[256,1024]{1,0:T(8,128)(2,1)S(1)}, u32[]{:S(2)}, u32[]{:S(2)}) collective-permute-start(bf16[256,1024]{1,0:T(8,128)(2,1)S(1)} %get-tuple-element.320), channel_id=1, source_target_pairs={{0,2},{2,4},{4,6},{6,8},{8,10},{10,12},{12,14},{1,3},{3,5},{5,7},{... | collective-permute-start | bytes 1572872 | tf_op jit(solution)/shard_map/ppermute | solution.py:26
  249.4 19.0 %all-to-all-start.7 = ((bf16[8,64,512]{2,1,0:T(8,128)(2,1)}), bf16[8,64,512]{2,1,0:T(8,128)(2,1)S(1)}, u32[]{:S(2)}, u32[]{:S(2)}) async-start(bf16[8,64,512]{2,1,0:T(8,128)(2,1)} %bitcast.36), calls=%async_computation.7 | async-start | bytes 1048576 | tf_op jit(solution)/shard_map/all_to_all | solution.py:173
  254.0 18.0 %copy-start.3 = (bf16[4,256,4,128]{1,3,2,0:T(8,128)(2,1)S(1)}, bf16[4,256,4,128]{1,3,2,0:T(8,128)(2,1)}, u32[]{:S(2)}) copy-start(bf16[4,256,4,128]{1,3,2,0:T(8,128)(2,1)} %get-tuple-element.102) | copy-start | bytes 3145732
  268.4 17.9 %all-to-all-start.6 = ((bf16[8,64,512]{2,1,0:T(8,128)(2,1)}), bf16[8,64,512]{2,1,0:T(8,128)(2,1)S(1)}, u32[]{:S(2)}, u32[]{:S(2)}) async-start(bf16[8,64,512]{2,1,0:T(8,128)(2,1)} %bitcast.34), calls=%async_computation.6 | async-start | bytes 1048576 | tf_op jit(solution)/shard_map/all_to_all | solution.py:170
  286.3 51.9 %all-to-all-start.5 = ((bf16[8,64,2048]{2,1,0:T(8,128)(2,1)}), bf16[8,64,2048]{2,1,0:T(8,128)(2,1)S(1)}, u32[]{:S(2)}, u32[]{:S(2)}) async-start(bf16[8,64,2048]{2,1,0:T(8,128)(2,1)} %bitcast.241), calls=%async_computation.5 | async-start | bytes 4194304 | tf_op jit(solution)/shard_map/all_to_all | solution.py:169
where the time goes:
time: 342 us; the launch traced here: 341 us
  waiting for transfers between devices  172 us (50%)
  local copies, waits for them, and re-layouts  70 us (20%)
  starting transfers between devices  55 us (16%)
  matrix products  36.7 us (11%)
  other arithmetic  5.9 us (2%)
    all_to_all x1, waiting for transfers between devices, local(): lax.all_to_all(gather_back(q_grad_own), 'seq', split_axis=0, concat_axis=...  44.5 us
    all_to_all x1, waiting for transfers between devices, local(): lax.all_to_all(pack_rows(out_grad), 'seq', split_axis=0, concat_axis=0, t...  29.7 us
    ppermute x1, waiting for transfers between devices, padded(): before = lax.ppermute(last, axis, up)  28.8 us
    ppermute x2, waiting for transfers between devices, from_behind(): return lax.ppermute(value, axis, pairs)  19.1 us
    scatter x6, local copies, waits for them, and re-layouts, unpack_rows(): return jnp.zeros((row_count, flat_rows.shape[1]), flat_rows.dtype).at[tar...  18.4 us
    scatter x4, local copies, waits for them, and re-layouts, pack_rows(): return jnp.zeros((slots, matrix.shape[1]), matrix.dtype).at[placed].set(m...  14.2 us
    all_to_all x1, starting transfers between devices, local(): lax.all_to_all(pack_rows(out_grad), 'seq', split_axis=0, concat_axis=0, t...  13.3 us
    all_to_all x1, waiting for transfers between devices, local(): lax.all_to_all(gather_back(kv_total[:, kv_width:]), 'seq', split_axis=0,...  11.8 us
  transfers between devices with their start and end apart: 12, of which 11 were waited for; matrix products, arithmetic and copies ran while one was open for 15% of the time, Pallas kernels for 0%

commit v1 on v0

--- a/solution.py
+++ b/solution.py
@@ -1,6 +1,10 @@
+import functools
+
 import jax
 import jax.numpy as jnp
 from jax import lax
+from jax.experimental import pallas as pl
+from jax.experimental.pallas import tpu as pltpu
 from jax.sharding import PartitionSpec as P
 
 HEAD_DIM = 128
@@ -30,7 +34,7 @@
     return matrix.reshape(matrix.shape[0], heads, -1).transpose(1, 0, 2)
 
 
-def local(queries, key_rows, value_rows, out_grad, owner_slot, block_links):
+def relay_plan(queries, key_rows, value_rows, out_grad, owner_slot, block_links):
     row_count = queries.shape[0]
     seq_count = lax.axis_size("seq")
     capacity = 4 * max(1, row_count // seq_count // 2)
@@ -181,6 +185,251 @@
     return (settle_rows(q_back), settle_rows(k_back), settle_rows(v_back))
 
 
+LOG2_E = 1.4426950408889634
+MASKED = -1e30
+NT = (((1,), (1,)), ((), ()))
+NN = (((1,), (0,)), ((), ()))
+
+
+def dot(a, b, dims):
+    return lax.dot_general(a, b, dims, preferred_element_type=jnp.float32)
+
+
+def flip(a):
+    return a.astype(jnp.float32).T.astype(jnp.bfloat16)
+
+
+def head_of(ref, j):
+    return ref[:, j * HEAD_DIM : (j + 1) * HEAD_DIM]
+
+
+def absorb(q_ref, shards, j, state):
+    factor = HEAD_DIM ** (-0.5) * LOG2_E
+    q = head_of(q_ref, j)
+    scores = [dot(k_ref[...], q, NT) * factor + bias_ref[...] for k_ref, _, bias_ref, _ in shards]
+    tops = [jnp.max(s, 0, keepdims=True) for s in scores]
+    top = functools.reduce(jnp.maximum, tops)
+    if state is not None:
+        top = jnp.maximum(top, state[0])
+    weights = [jnp.exp2(s - top) for s in scores]
+    total = sum(jnp.sum(w, 0, keepdims=True) for w in weights)
+    mixed = sum(dot(s[3], w.astype(jnp.bfloat16), NN) for s, w in zip(shards, weights))
+    if state is not None:
+        keep = jnp.exp2(state[0] - top)
+        total = total + state[1] * keep
+        mixed = mixed + state[2] * keep
+    return top, total, mixed
+
+
+def backprop(q_ref, g_ref, shard, group, norm, delta, q_sums):
+    k_ref, v_ref, bias_ref, k_flip = shard
+    scale = HEAD_DIM ** (-0.5)
+    k_grad, v_grad = 0.0, 0.0
+    for j in range(group):
+        q, g = head_of(q_ref, j), head_of(g_ref, j)
+        w = jnp.exp2(dot(k_ref[...], q, NT) * (scale * LOG2_E) + bias_ref[...] - norm[j])
+        d_probs = dot(v_ref[...], g, NT)
+        d_scores = (w * (d_probs - delta[j])).astype(jnp.bfloat16)
+        k_grad = k_grad + dot(d_scores, q, NN)
+        v_grad = v_grad + dot(w.astype(jnp.bfloat16), g, NN)
+        term = dot(k_flip, d_scores, NN)
+        q_sums[j] = term if q_sums[j] is None else q_sums[j] + term
+    return k_grad * scale, v_grad
+
+
+def rows_of(ref, group):
+    return [ref[j : j + 1, :] for j in range(group)]
+
+
+def forward_kernel(count, group, first, q_ref, *refs):
+    shards = [refs[3 * i : 3 * i + 3] for i in range(count)]
+    refs = refs[3 * count :]
+    if not first:
+        top_in, total_in, mixed_in = refs[:3]
+        refs = refs[3:]
+    top_out, total_out, mixed_out = refs
+    shards = [(k, v, b, flip(v[...])) for k, v, b in shards]
+    for j in range(group):
+        state = None if first else (top_in[j : j + 1, :], total_in[j : j + 1, :], mixed_in[j])
+        top, total, mixed = absorb(q_ref, shards, j, state)
+        top_out[j : j + 1, :] = top
+        total_out[j : j + 1, :] = total
+        mixed_out[j] = mixed
+
+
+def turn_kernel(group, q_ref, g_ref, k_ref, v_ref, bias_ref, top_in, total_in, mixed_in, norm_out, delta_out, q_out, grads_out):
+    shards = [(k_ref, v_ref, bias_ref, flip(v_ref[...]))]
+    norm, delta = [], []
+    for j in range(group):
+        state = (top_in[j : j + 1, :], total_in[j : j + 1, :], mixed_in[j])
+        top, total, mixed = absorb(q_ref, shards, j, state)
+        attended = (mixed / total).astype(jnp.bfloat16).astype(jnp.float32)
+        norm.append(top + jnp.log2(total))
+        delta.append(jnp.sum(head_of(g_ref, j).astype(jnp.float32).T * attended, 0, keepdims=True))
+        norm_out[j : j + 1, :] = norm[j]
+        delta_out[j : j + 1, :] = delta[j]
+    q_sums = [None] * group
+    k_grad, v_grad = backprop(q_ref, g_ref, (k_ref, v_ref, bias_ref, flip(k_ref[...])), group, norm, delta, q_sums)
+    grads_out[0] = k_grad.astype(jnp.bfloat16)
+    grads_out[1] = v_grad.astype(jnp.bfloat16)
+    for j in range(group):
+        q_out[j] = q_sums[j]
+
+
+def backward_kernel(count, group, last, q_ref, g_ref, *refs):
+    shards = [refs[3 * i : 3 * i + 3] for i in range(count)]
+    norm_ref, delta_ref, q_in, q_out = refs[3 * count : 3 * count + 4]
+    grads_out = refs[3 * count + 4 :]
+    norm, delta = rows_of(norm_ref, group), rows_of(delta_ref, group)
+    q_sums = [q_in[j] for j in range(group)]
+    for (k_ref, v_ref, bias_ref), out in zip(shards, grads_out):
+        shard = (k_ref, v_ref, bias_ref, flip(k_ref[...]))
+        out[0], out[1] = backprop(q_ref, g_ref, shard, group, norm, delta, q_sums)
+    for j in range(group):
+        if last:
+            q_out[:, j * HEAD_DIM : (j + 1) * HEAD_DIM] = (q_sums[j].T * HEAD_DIM ** (-0.5)).astype(jnp.bfloat16)
+        else:
+            q_out[j] = q_sums[j]
+
+
+def gather_plan(queries, key_rows, value_rows, out_grad, owner_slot, block_links):
+    rows = queries.shape[0]
+    peers = lax.axis_size("seq")
+    half = peers // 2
+    width = key_rows.shape[1]
+    heads = width // HEAD_DIM
+    group = queries.shape[1] // width
+    ring = list(range(0, peers, 2)) + list(range(peers - 1, 0, -2))
+    onward = [(ring[i], ring[(i + 1) % peers]) for i in range(peers)]
+    back = [(b, a) for a, b in onward]
+
+    def send_on(value):
+        return lax.ppermute(value, "seq", onward)
+
+    def send_back(value):
+        return lax.ppermute(value, "seq", back)
+
+    own = jnp.stack([key_rows, value_rows])
+    behind, ahead = [own], [own]
+    for _ in range(half - 1):
+        behind.append(send_on(behind[-1]))
+        ahead.append(send_back(ahead[-1]))
+    far = (send_on(behind[-1][0]), send_back(ahead[-1][1]))
+
+    blocks = peers * rows // BLOCK
+    span = block_links.shape[1]
+    notes = lax.all_gather(jnp.concatenate([owner_slot, block_links.reshape(-1)]), "seq")
+    links = notes[:, rows:].reshape(blocks, span)
+    ids = jnp.arange(blocks, dtype=jnp.int32)
+    place = jnp.array([ring.index(i) for i in range(peers)], jnp.int32)[lax.axis_index("seq")]
+    order = jnp.array(ring, jnp.int32)[(place - jnp.arange(peers, dtype=jnp.int32)) % peers]
+    key_block = notes[order, :rows] // BLOCK
+    reach = ids[None, :, None] - ids[:, None, None] + span // 2 == jnp.arange(span, dtype=jnp.int32)
+    linked = jnp.sum(jnp.where(reach, links[:, None, :], 0), 2).astype(jnp.bfloat16)
+    query_hot = (ids[:, None] == (owner_slot // BLOCK)[None, :]).astype(jnp.bfloat16)
+    key_hot = (key_block[:, :, None] == ids).astype(jnp.bfloat16)
+    query_links = dot(linked, query_hot, (((0,), (0,)), ((), ()))).astype(jnp.bfloat16)
+    allowed = dot(key_hot.reshape(peers * rows, blocks), query_links, NN)
+    bias = jnp.where(allowed > 0.5, 0.0, MASKED).reshape(peers, rows, rows)
+
+    f32 = jnp.float32
+    wide = pl.BlockSpec((rows, group * HEAD_DIM), lambda h: (0, h))
+    line = pl.BlockSpec((None, group, rows), lambda h: (h, 0, 0))
+    tall = pl.BlockSpec((None, group, HEAD_DIM, rows), lambda h: (h, 0, 0, 0))
+    pair = pl.BlockSpec((2, rows, HEAD_DIM), lambda h: (0, 0, h))
+    lines = jax.ShapeDtypeStruct((heads, group, rows), f32)
+    talls = jax.ShapeDtypeStruct((heads, group, HEAD_DIM, rows), f32)
+
+    def pairs(dtype):
+        return jax.ShapeDtypeStruct((2, rows, width), dtype)
+
+    def shard_args(shard, at):
+        mask = (bias, pl.BlockSpec((None, rows, rows), lambda h: (at, 0, 0)))
+        if isinstance(shard, tuple):
+            narrow = pl.BlockSpec((rows, HEAD_DIM), lambda h: (0, h))
+            return [(shard[0], narrow), (shard[1], narrow), mask]
+        return [
+            (shard, pl.BlockSpec((None, rows, HEAD_DIM), lambda h: (0, 0, h))),
+            (shard, pl.BlockSpec((None, rows, HEAD_DIM), lambda h: (1, 0, h))),
+            mask,
+        ]
+
+    def call(kernel, args, outs, products, aliases):
+        flops = 2 * products * heads * group * rows * rows * HEAD_DIM
+        moved = sum(2 * rows * width * 4 for _ in args)
+        return pl.pallas_call(
+            kernel,
+            grid=(heads,),
+            in_specs=[spec for _, spec in args],
+            out_specs=[spec for _, spec in outs],
+            out_shape=[shape for shape, _ in outs],
+            input_output_aliases=aliases,
+            cost_estimate=pl.CostEstimate(
+                flops=flops, bytes_accessed=moved, transcendentals=products * heads * group * rows * rows // 2
+            ),
+            compiler_params=pltpu.CompilerParams(vmem_limit_bytes=48 * 1024 * 1024),
+        )(*[value for value, _ in args])
+
+    def forward(shards, state):
+        first = state is None
+        args = [(queries, wide)] + [a for shard, at in shards for a in shard_args(shard, at)]
+        at = len(args)
+        if not first:
+            args += list(zip(state, (line, line, tall)))
+        kernel = functools.partial(forward_kernel, len(shards), group, first)
+        aliases = {} if first else {at + i: i for i in range(3)}
+        return call(kernel, args, [(lines, line), (lines, line), (talls, tall)], 2 * len(shards), aliases)
+
+    def backward(shards, norm, delta, q_sums, last):
+        args = [(queries, wide), (out_grad, wide)] + [a for shard, at in shards for a in shard_args(shard, at)]
+        args += [(norm, line), (delta, line), (q_sums, tall)]
+        kernel = functools.partial(backward_kernel, len(shards), group, last)
+        q_out = (jax.ShapeDtypeStruct(queries.shape, queries.dtype), wide) if last else (talls, tall)
+        outs = [q_out] + [(pairs(f32), pair) for _ in shards]
+        return call(kernel, args, outs, 5 * len(shards), {} if last else {len(args) - 1: 0})
+
+    state = forward([(own, 0)], None)
+    for r in range(1, half):
+        state = forward([(behind[r], r), (ahead[r], peers - r)], state)
+    args = [(queries, wide), (out_grad, wide)] + shard_args(far, half)
+    args += list(zip(state, (line, line, tall)))
+    norm, delta, q_sums, far_grads = call(
+        functools.partial(turn_kernel, group),
+        args,
+        [(lines, line), (lines, line), (talls, tall), (pairs(jnp.bfloat16), pair)],
+        7,
+        {5: 0, 6: 1, 7: 2},
+    )
+    from_ahead, from_behind_ = send_back(far_grads[0]), send_on(far_grads[1])
+    for r in range(half - 1, 0, -1):
+        q_sums, low, high = backward([(behind[r], r), (ahead[r], peers - r)], norm, delta, q_sums, False)
+        if r == half - 1:
+            low = jnp.stack([low[0] + from_ahead.astype(f32), low[1]])
+            high = jnp.stack([high[0], high[1] + from_behind_.astype(f32)])
+        else:
+            low = low + from_ahead.astype(f32)
+            high = high + from_behind_.astype(f32)
+        from_ahead, from_behind_ = send_back(low.astype(jnp.bfloat16)), send_on(high.astype(jnp.bfloat16))
+    query_grad, mine = backward([(own, 0)], norm, delta, q_sums, True)
+    if half == 1:
+        total = jnp.stack([mine[0] + from_ahead.astype(f32), mine[1] + from_behind_.astype(f32)])
+    else:
+        total = mine + from_ahead.astype(f32) + from_behind_.astype(f32)
+    total = total.astype(jnp.bfloat16)
+    return query_grad, total[0], total[1]
+
+
+def local(queries, key_rows, value_rows, out_grad, owner_slot, block_links):
+    rows = queries.shape[0]
+    peers = lax.axis_size("seq")
+    q_width, kv_width = queries.shape[1], key_rows.shape[1]
+    slots = 4 * peers * max(1, rows // peers // 2)
+    gathered = 2 * (peers - 1) * rows * 2 * kv_width
+    relayed = slots * (3 * q_width + 4 * kv_width) + 4 * rows * 2 * kv_width
+    plan = gather_plan if peers % 2 == 0 and gathered <= relayed else relay_plan
+    return plan(queries, key_rows, value_rows, out_grad, owner_slot, block_links)
+
+
 def solution(mesh):
     return jax.shard_map(
         local,

time: 342 us -> 183 us (0.54)
  waiting for transfers between devices: 172 us -> 13.6 us
  Pallas kernels: 0 us -> 78.9 us
  local copies, waits for them, and re-layouts: 70 us -> 27.2 us
  blocking collectives: 0 us -> 37.7 us
  starting transfers between devices: 55 us -> 17.6 us
  matrix products: 36.7 us -> 0.59 us
    all_to_all x8 -> x0, waiting for transfers between devices: 124 us -> none  [the longest x1 44.5 us: local(): lax.all_to_all(gather_back(q_grad_own), 'seq', split_axis=0, concat_axis=...]
    pallas_call x0 -> x9, Pallas kernels: none -> 78.9 us  [call(): pl.pallas_call(kernel, grid=(heads,), in_specs=[spec for _, spec in args]...]
    all_to_all x8 -> x0, starting transfers between devices: 44.1 us -> none  [the longest x1 13.3 us: local(): lax.all_to_all(pack_rows(out_grad), 'seq', split_axis=0, concat_axis=0, t...]
    unnamed x0 -> x1, blocking collectives: none -> 37.7 us
    dot_general x28 -> x1, matrix products: 36.7 us -> 0.59 us  [dot(): return lax.dot_general(a, b, dims, preferred_element_type=jnp.float32)]
    ppermute x4 -> x16, waiting for transfers between devices: 47.9 us -> 13.6 us  [the longest x8 13.1 us: send_on(): return lax.ppermute(value, 'seq', onward)]
    scatter x11 -> x0, local copies, waits for them, and re-layouts: 33.9 us -> none  [the longest x6 18.4 us: unpack_rows(): return jnp.zeros((row_count, flat_rows.shape[1]), flat_rows.dtype).at[tar...]
    ppermute x4 -> x16, starting transfers between devices: 11 us -> 17.6 us  [the longest x8 11.5 us: send_on(): return lax.ppermute(value, 'seq', onward)]
  transfers between devices with their start and end apart: 12 -> 16, of which waited for: 11 -> 4; matrix products, arithmetic and copies ran while one was open for 15% -> 14% of each run, Pallas kernels for 0% -> 38%
where the time goes in v1:
time: 183 us; the launch traced here: 182 us
  Pallas kernels  78.9 us (43%)
  blocking collectives  37.7 us (21%)
  local copies, waits for them, and re-layouts  27.2 us (15%)
  starting transfers between devices  17.6 us (10%)
  waiting for transfers between devices  13.6 us (7%)
  other arithmetic  4.52 us (2%)
    pallas_call x9, Pallas kernels, call(): pl.pallas_call(kernel, grid=(heads,), in_specs=[spec for _, spec in args]...  78.9 us
    unnamed x1, blocking collectives  37.7 us
    gather x32, local copies, waits for them, and re-layouts  15.1 us
    ppermute x8, waiting for transfers between devices, send_on(): return lax.ppermute(value, 'seq', onward)  13.1 us
    ppermute x8, starting transfers between devices, send_on(): return lax.ppermute(value, 'seq', onward)  11.5 us
    ppermute x8, starting transfers between devices, send_back(): return lax.ppermute(value, 'seq', back)  6.1 us
    unnamed x27, local copies, waits for them, and re-layouts  5.64 us
  transfers between devices with their start and end apart: 16, of which 4 were waited for; matrix products, arithmetic and copies ran while one was open for 14% of the time, Pallas kernels for 38%

profile of v1, /device:TPU:0, one launch (start us, length us, event | category | flops | bytes accessed | tf_op | source)
XLA Modules:
  0.0 181.9 jit_solution(8720209691876163034)
XLA Ops:
  0.6 1.2 pad_maximum_fusion.refs_0_.refs_1_
  1.8 3.0 %collective-permute-start.4 = (bf16[2,256,512]{2,1,0:T(8,128)(2,1)S(1)}, bf16[2,256,512]{2,1,0:T(8,128)(2,1)S(1)}, u32[]{:S(2)}, u32[]{:S(2)}) collective-permute-start(bf16[2,256,512]{2,1,0:T(8,128)(2,1)S(1)} %pad_maximum_fusion.refs_0_.refs_1_), channel_id=1, source_target_pairs={{4,0},{8,4},{12,8},{14,12},{10,14},{6,10},{2,6},{0,2},{5,1},{9,5},... | collective-permute-start | bytes 1572872 | tf_op jit(solution)/shard_map/ppermute | solution.py:310
  5.0 0.8 reshape.114
  5.7 1.2 dynamic_slice.3
  7.0 0.7 fusion.13
  7.6 1.3 gather_fusion
  9.0 1.2 dynamic-slice.3
  10.9 0.8 add_dynamic-update-slice_fusion
  11.7 37.7 %all-reduce.1 = s32[2128]{0:T(1024)S(1)} all-reduce(s32[2128]{0:T(1024)S(1)} %add_dynamic-update-slice_fusion), channel_id=2, replica_groups=mesh['parts'=2,'seq'=8,'head'=2] {'seq'}, use_global_device_ids=true, to_apply=%add.1 | all-reduce | flops 2128 | bytes 17024
  49.6 0.8 copy-done.8
  50.4 15.2 %while.1 = (s32[]{:T(128)}, s32[8,266]{1,0:T(8,128)S(1)}, s32[8,2]{0,1:T(2,128)S(1)}, s32[8,256]{1,0:T(8,128)S(1)}, s32[]{:T(128)}, /*index=5*/s32[]{:T(128)}) while((s32[]{:T(128)}, s32[8,266]{1,0:T(8,128)S(1)}, s32[8,2]{0,1:T(2,128)S(1)}, s32[8,256]{1,0:T(8,128)S(1)}, s32[]{:T(128)}, /*index=5*/s32[]{:T(128)}) %tuple.25), condition=%wide.while_cond, body=%wide.while_body.sunk | while | flops 2 | bytes 4217 | solution.py:326
  51.0 1.3 dynamic-slice.8
  52.9 1.3 dynamic-slice.8
  54.8 1.3 dynamic-slice.8
  56.7 1.3 dynamic-slice.8
  58.6 1.3 dynamic-slice.8
  60.5 1.3 dynamic-slice.8
  62.4 1.3 dynamic-slice.8
  64.3 1.3 dynamic-slice.8
  65.8 2.1 %collective-permute-start.1 = (bf16[2,256,512]{2,1,0:T(8,128)(2,1)S(1)}, bf16[2,256,512]{2,1,0:T(8,128)(2,1)}, u32[]{:S(2)}, u32[]{:S(2)}) collective-permute-start(bf16[2,256,512]{2,1,0:T(8,128)(2,1)S(1)} %collective-permute-done.refs_0_.refs_1_), channel_id=1, source_target_pairs={{0,4},{4,8},{8,12},{12,14},{14,10},{10,6},{6,2},{2,0},{1,5},{5,9},... | collective-permute-start | bytes 1572872 | tf_op jit(solution)/shard_map/ppermute | solution.py:307
  67.9 0.8 copy-done.10
  68.9 0.7 and_select_fusion
  69.6 10.8 %collective-permute-done.1.refs_0_.refs_1_ = bf16[2,256,512]{2,1,0:T(8,128)(2,1)} collective-permute-done((bf16[2,256,512]{2,1,0:T(8,128)(2,1)S(1)}, bf16[2,256,512]{2,1,0:T(8,128)(2,1)}, u32[]{:S(2)}, u32[]{:S(2)}) %collective-permute-start.1) | collective-permute-done | bytes 524320 | tf_op jit(solution)/shard_map/ppermute | solution.py:307
  80.4 1.7 collective-permute-start.2
  82.8 1.4 copy-done.6
  84.2 5.4 %shard_map.103 = (f32[4,4,256]{2,1,0:T(4,128)S(1)}, f32[4,4,256]{2,1,0:T(4,128)S(1)}, f32[4,4,128,256]{3,2,1,0:T(8,128)S(1)}) custom-call(bf16[256,2048]{1,0:T(8,128)(2,1)S(1)} %copy-done.3, bf16[2,256,512]{2,1,0:T(8,128)(2,1)S(1)} %copy-done.6, bf16[2,256,512]{2,1,0:T(8,128)(2,1)S(1)} %copy-done.6, f32[8,256,256]{2,1,0:T(8,128)S(1)} %bitcast.45), custom_call_target="tpu_custom_call" | custom-call | flops 536870912 | bytes 4194304 | tf_op jit(solution)/shard_map/pallas_call | solution.py:360
  89.6 1.0 slice_bitcast_fusion.2
  90.9 1.4 collective-permute-done.2.refs_0_.refs_1_
  92.3 1.0 slice_bitcast_fusion.3
  93.3 1.5 collective-permute-start.3
  94.8 7.7 %shard_map.104 = (f32[4,4,256]{2,1,0:T(4,128)S(1)}, f32[4,4,256]{2,1,0:T(4,128)S(1)}, f32[4,4,128,256]{3,2,1,0:T(8,128)S(1)}) custom-call(bf16[256,2048]{1,0:T(8,128)(2,1)S(1)} %copy-done.3, bf16[2,256,512]{2,1,0:T(8,128)(2,1)S(1)} %copy-done.11, bf16[2,256,512]{2,1,0:T(8,128)(2,1)S(1)} %copy-done.11, ...), custom_call_target="tpu_custom_call", output_to_operand_aliasing={{0}: (7, {}), {1}: (8, {}), {2}: (9, {})} | custom-call | flops 1073741824 | bytes 10485760 | tf_op jit(solution)/shard_map/pallas_call | solution.py:360
  102.5 7.8 %shard_map.105 = (f32[4,4,256]{2,1,0:T(4,128)S(1)}, f32[4,4,256]{2,1,0:T(4,128)S(1)}, f32[4,4,128,256]{3,2,1,0:T(8,128)S(1)}) custom-call(bf16[256,2048]{1,0:T(8,128)(2,1)S(1)} %copy-done.3, bf16[2,256,512]{2,1,0:T(8,128)(2,1)} %collective-permute-done.1.refs_0_.refs_1_, ...), custom_call_target="tpu_custom_call", output_to_operand_aliasing={{0}: (7, {}), {1}: (8, {}), {2}: (9, {})} | custom-call | flops 1073741824 | bytes 10485760 | tf_op jit(solution)/shard_map/pallas_call | solution.py:360
  110.3 7.8 %shard_map.106 = (f32[4,4,256]{2,1,0:T(4,128)S(1)}, f32[4,4,256]{2,1,0:T(4,128)S(1)}, f32[4,4,128,256]{3,2,1,0:T(8,128)S(1)}) custom-call(bf16[256,2048]{1,0:T(8,128)(2,1)S(1)} %copy-done.3, bf16[2,256,512]{2,1,0:T(8,128)(2,1)} %collective-permute-done.2.refs_0_.refs_1_, ...), custom_call_target="tpu_custom_call", output_to_operand_aliasing={{0}: (7, {}), {1}: (8, {}), {2}: (9, {})} | custom-call | flops 1073741824 | bytes 10485760 | tf_op jit(solution)/shard_map/pallas_call | solution.py:360
  118.2 10.4 %shard_map.107 = (f32[4,4,256]{2,1,0:T(4,128)S(1)}, f32[4,4,256]{2,1,0:T(4,128)S(1)}, f32[4,4,128,256]{3,2,1,0:T(8,128)S(1)}, bf16[2,256,512]{2,1,0:T(8,128)(2,1)S(1)}) custom-call(bf16[256,2048]{1,0:T(8,128)(2,1)S(1)} %copy-done.3, bf16[256,2048]{1,0:T(8,128)(2,1)S(1)} %copy-done.4, ...), custom_call_target="tpu_custom_call", output_to_operand_aliasing={{0}: (5, {}), {1}: (6, {}), {2}: (7, {})} | custom-call | flops 1879048192 | bytes 8388608 | tf_op jit(solution)/shard_map/pallas_call | solution.py:360
  128.6 1.3 copy-done.2
  130.6 1.4 collective-permute-start.12
  132.1 11.0 %shard_map.108 = (f32[4,4,128,256]{3,2,1,0:T(8,128)}, f32[2,256,512]{2,1,0:T(8,128)S(1)}, f32[2,256,512]{2,1,0:T(8,128)S(1)}) custom-call(bf16[256,2048]{1,0:T(8,128)(2,1)S(1)} %copy-done.3, bf16[256,2048]{1,0:T(8,128)(2,1)S(1)} %copy-done.4, bf16[2,256,512]{2,1,0:T(8,128)(2,1)} %collective-permute-done.2.refs_0_.refs_1_, ...), custom_call_target="tpu_custom_call", output_to_operand_aliasing={{0}: (10, {})} | custom-call | flops 2684354560 | bytes 11534336 | tf_op jit(solution)/shard_map/pallas_call | solution.py:360
  143.3 0.7 collective-permute-start.9
  144.1 1.7 collective-permute-start.13
  145.7 11.0 %shard_map.109 = (f32[4,4,128,256]{3,2,1,0:T(8,128)}, f32[2,256,512]{2,1,0:T(8,128)S(1)}, f32[2,256,512]{2,1,0:T(8,128)S(1)}) custom-call(bf16[256,2048]{1,0:T(8,128)(2,1)S(1)} %copy-done.3, bf16[256,2048]{1,0:T(8,128)(2,1)S(1)} %copy-done.4, bf16[2,256,512]{2,1,0:T(8,128)(2,1)} %collective-permute-done.1.refs_0_.refs_1_, ...), custom_call_target="tpu_custom_call", output_to_operand_aliasing={{0}: (10, {})} | custom-call | flops 2684354560 | bytes 11534336 | tf_op jit(solution)/shard_map/pallas_call | solution.py:360
  157.3 0.7 collective-permute-start.10
  158.2 1.5 collective-permute-start.14
  159.6 11.0 %shard_map.110 = (f32[4,4,128,256]{3,2,1,0:T(8,128)}, f32[2,256,512]{2,1,0:T(8,128)S(1)}, f32[2,256,512]{2,1,0:T(8,128)S(1)}) custom-call(bf16[256,2048]{1,0:T(8,128)(2,1)S(1)} %copy-done.3, bf16[256,2048]{1,0:T(8,128)(2,1)S(1)} %copy-done.4, bf16[2,256,512]{2,1,0:T(8,128)(2,1)S(1)} %copy-done.11, ...), custom_call_target="tpu_custom_call", output_to_operand_aliasing={{0}: (10, {})} | custom-call | flops 2684354560 | bytes 11534336 | tf_op jit(solution)/shard_map/pallas_call | solution.py:360
  170.8 0.7 collective-permute-start.11
  171.6 1.5 collective-permute-start.15
  173.1 6.9 %shard_map.111 = (bf16[256,2048]{1,0:T(8,128)(2,1)}, f32[2,256,512]{2,1,0:T(8,128)S(1)}) custom-call(bf16[256,2048]{1,0:T(8,128)(2,1)S(1)} %copy-done.3, bf16[256,2048]{1,0:T(8,128)(2,1)S(1)} %copy-done.4, bf16[2,256,512]{2,1,0:T(8,128)(2,1)S(1)} %copy-done.7, bf16[2,256,512]{2,1,0:T(8,128)(2,1)S(1)} %copy-done.7, f32[8,256,256]{2,1,0:T(8,128)S(1)} %bitcast.59, ...), custom_call_target="tpu_custom_call" | custom-call | flops 1342177280 | bytes 8388608 | tf_op jit(solution)/shard_map/pallas_call | solution.py:360
  180.0 0.8 collective-permute-done.15
  181.1 0.8 slice_bitcast_fusion
  (88 shorter events, 9.0 us)
Async XLA Ops:
  0.6 82.1 %copy-start.3 = (bf16[256,2048]{1,0:T(8,128)(2,1)S(1)}, bf16[256,2048]{1,0:T(8,128)(2,1)}, u32[]{:S(2)}) copy-start(bf16[256,2048]{1,0:T(8,128)(2,1)} %q_ref.17) | copy-start | bytes 3145732
  1.8 78.6 %copy-start.5 = (bf16[2,256,512]{2,1,0:T(8,128)(2,1)}, bf16[2,256,512]{2,1,0:T(8,128)(2,1)S(1)}, u32[]{:S(2)}) copy-start(bf16[2,256,512]{2,1,0:T(8,128)(2,1)S(1)} %pad_maximum_fusion.refs_0_.refs_1_) | copy-start | bytes 1572868
  1.8 47.7 %collective-permute-start.4 = (bf16[2,256,512]{2,1,0:T(8,128)(2,1)S(1)}, bf16[2,256,512]{2,1,0:T(8,128)(2,1)S(1)}, u32[]{:S(2)}, u32[]{:S(2)}) collective-permute-start(bf16[2,256,512]{2,1,0:T(8,128)(2,1)S(1)} %pad_maximum_fusion.refs_0_.refs_1_), channel_id=1, source_target_pairs={{4,0},{8,4},{12,8},{14,12},{10,14},{6,10},{2,6},{0,2},{5,1},{9,5},... | collective-permute-start | bytes 1572872 | tf_op jit(solution)/shard_map/ppermute | solution.py:310
  4.8 61.0 %collective-permute-start = (bf16[2,256,512]{2,1,0:T(8,128)(2,1)S(1)}, bf16[2,256,512]{2,1,0:T(8,128)(2,1)S(1)}, u32[]{:S(2)}, u32[]{:S(2)}) collective-permute-start(bf16[2,256,512]{2,1,0:T(8,128)(2,1)S(1)} %pad_maximum_fusion.refs_0_.refs_1_), channel_id=1, source_target_pairs={{0,4},{4,8},{8,12},{12,14},{14,10},{10,6},{6,2},{2,0},{1,5},{5,9},... | collective-permute-start | bytes 1572872 | tf_op jit(solution)/shard_map/ppermute | solution.py:307
  49.5 19.3 %collective-permute-start.5 = (bf16[2,256,512]{2,1,0:T(8,128)(2,1)S(1)}, bf16[2,256,512]{2,1,0:T(8,128)(2,1)}, u32[]{:S(2)}, u32[]{:S(2)}) collective-permute-start(bf16[2,256,512]{2,1,0:T(8,128)(2,1)S(1)} %collective-permute-done.4.refs_3_.refs_4_), channel_id=1, source_target_pairs={{4,0},{8,4},{12,8},{14,12},{10,14},{6,10},{2,6},{0,2},{5,1},{9,5},... | collective-permute-start | bytes 1572872 | tf_op jit(solution)/shard_map/ppermute | solution.py:310
  49.6 0.8 copy-start.8
  65.8 14.6 %collective-permute-start.1 = (bf16[2,256,512]{2,1,0:T(8,128)(2,1)S(1)}, bf16[2,256,512]{2,1,0:T(8,128)(2,1)}, u32[]{:S(2)}, u32[]{:S(2)}) collective-permute-start(bf16[2,256,512]{2,1,0:T(8,128)(2,1)S(1)} %collective-permute-done.refs_0_.refs_1_), channel_id=1, source_target_pairs={{0,4},{4,8},{8,12},{12,14},{14,10},{10,6},{6,2},{2,0},{1,5},{5,9},... | collective-permute-start | bytes 1572872 | tf_op jit(solution)/shard_map/ppermute | solution.py:307
  67.9 0.8 copy-start.10
  68.8 20.8 %collective-permute-start.6 = (bf16[2,256,512]{2,1,0:T(8,128)(2,1)}, bf16[2,256,512]{2,1,0:T(8,128)(2,1)}, u32[]{:S(2)}, u32[]{:S(2)}) collective-permute-start(bf16[2,256,512]{2,1,0:T(8,128)(2,1)} %collective-permute-done.5.refs_3_.refs_4_), channel_id=1, source_target_pairs={{4,0},{8,4},{12,8},{14,12},{10,14},{6,10},{2,6},{0,2},{5,1},{9,5},... | collective-permute-start | bytes 1572872 | tf_op jit(solution)/shard_map/ppermute | solution.py:310
  80.4 11.9 %collective-permute-start.2 = (bf16[2,256,512]{2,1,0:T(8,128)(2,1)}, bf16[2,256,512]{2,1,0:T(8,128)(2,1)}, u32[]{:S(2)}, u32[]{:S(2)}) collective-permute-start(bf16[2,256,512]{2,1,0:T(8,128)(2,1)} %collective-permute-done.1.refs_0_.refs_1_), channel_id=1, source_target_pairs={{0,4},{4,8},{8,12},{12,14},{14,10},{10,6},{6,2},{2,0},{1,5},{5,9},... | collective-permute-start | bytes 1572872 | tf_op jit(solution)/shard_map/ppermute | solution.py:307
  82.7 6.9 %copy-start = (f32[2048,256]{1,0:T(8,128)}, f32[2048,256]{1,0:T(8,128)S(1)}, u32[]{:S(2)}) copy-start(f32[2048,256]{1,0:T(8,128)S(1)} %fusion) | copy-start | bytes 6291460
  82.7 1.4 copy-start.6
  84.2 10.6 %copy-start.9 = (bf16[2,256,512]{2,1,0:T(8,128)(2,1)S(1)}, bf16[2,256,512]{2,1,0:T(8,128)(2,1)}, u32[]{:S(2)}) copy-start(bf16[2,256,512]{2,1,0:T(8,128)(2,1)} %copy-done.8) | copy-start | bytes 1572868
  84.2 10.6 %copy-start.11 = (bf16[2,256,512]{2,1,0:T(8,128)(2,1)S(1)}, bf16[2,256,512]{2,1,0:T(8,128)(2,1)}, u32[]{:S(2)}) copy-start(bf16[2,256,512]{2,1,0:T(8,128)(2,1)} %copy-done.10) | copy-start | bytes 1572868
  90.6 27.6 %collective-permute-start.7 = (bf16[256,512]{1,0:T(8,128)(2,1)S(1)}, bf16[256,512]{1,0:T(8,128)(2,1)S(1)}, u32[]{:S(2)}, u32[]{:S(2)}) collective-permute-start(bf16[256,512]{1,0:T(8,128)(2,1)S(1)} %slice_bitcast_fusion.2), channel_id=1, source_target_pairs={{4,0},{8,4},{12,8},{14,12},{10,14},{6,10},{2,6},{0,2},{5,1},{9,5},... | collective-permute-start | bytes 786440 | tf_op jit(solution)/shard_map/ppermute | solution.py:310
  93.3 24.9 %collective-permute-start.3 = (bf16[256,512]{1,0:T(8,128)(2,1)S(1)}, bf16[256,512]{1,0:T(8,128)(2,1)S(1)}, u32[]{:S(2)}, u32[]{:S(2)}) collective-permute-start(bf16[256,512]{1,0:T(8,128)(2,1)S(1)} %slice_bitcast_fusion.3), channel_id=1, source_target_pairs={{0,4},{4,8},{8,12},{12,14},{14,10},{10,6},{6,2},{2,0},{1,5},{5,9},... | collective-permute-start | bytes 786440 | tf_op jit(solution)/shard_map/ppermute | solution.py:307
  110.3 7.9 %copy-start.4 = (bf16[256,2048]{1,0:T(8,128)(2,1)S(1)}, bf16[256,2048]{1,0:T(8,128)(2,1)}, u32[]{:S(2)}) copy-start(bf16[256,2048]{1,0:T(8,128)(2,1)} %g_ref.9) | copy-start | bytes 3145732
  128.6 1.3 copy-start.2
  130.0 13.2 %collective-permute-start.8 = (bf16[256,512]{1,0:T(8,128)(2,1)S(1)}, bf16[256,512]{1,0:T(8,128)(2,1)S(1)}, u32[]{:S(2)}, u32[]{:S(2)}) collective-permute-start(bf16[256,512]{1,0:T(8,128)(2,1)S(1)} %get-tuple-element.77), channel_id=1, source_target_pairs={{4,0},{8,4},{12,8},{14,12},{10,14},{6,10},{2,6},{0,2},{5,1},{9,5},... | collective-permute-start | bytes 786440 | tf_op jit(solution)/shard_map/ppermute | solution.py:310
  130.6 13.3 %collective-permute-start.12 = (bf16[256,512]{1,0:T(8,128)(2,1)S(1)}, bf16[256,512]{1,0:T(8,128)(2,1)S(1)}, u32[]{:S(2)}, u32[]{:S(2)}) collective-permute-start(bf16[256,512]{1,0:T(8,128)(2,1)S(1)} %get-tuple-element.78), channel_id=1, source_target_pairs={{0,4},{4,8},{8,12},{12,14},{14,10},{10,6},{6,2},{2,0},{1,5},{5,9},... | collective-permute-start | bytes 786440 | tf_op jit(solution)/shard_map/ppermute | solution.py:307
  143.3 13.9 %collective-permute-start.9 = (bf16[2,256,512]{2,1,0:T(8,128)(2,1)S(1)}, bf16[2,256,512]{2,1,0:T(8,128)(2,1)S(1)}, u32[]{:S(2)}, u32[]{:S(2)}) collective-permute-start(bf16[2,256,512]{2,1,0:T(8,128)(2,1)S(1)} %pad_maximum_fusion.1), channel_id=1, source_target_pairs={{4,0},{8,4},{12,8},{14,12},{10,14},{6,10},{2,6},{0,2},{5,1},{9,5},... | collective-permute-start | bytes 1572872 | tf_op jit(solution)/shard_map/ppermute | solution.py:310
  144.1 13.9 %collective-permute-start.13 = (bf16[2,256,512]{2,1,0:T(8,128)(2,1)S(1)}, bf16[2,256,512]{2,1,0:T(8,128)(2,1)S(1)}, u32[]{:S(2)}, u32[]{:S(2)}) collective-permute-start(bf16[2,256,512]{2,1,0:T(8,128)(2,1)S(1)} %pad_maximum_fusion.2), channel_id=1, source_target_pairs={{0,4},{4,8},{8,12},{12,14},{14,10},{10,6},{6,2},{2,0},{1,5},{5,9},... | collective-permute-start | bytes 1572872 | tf_op jit(solution)/shard_map/ppermute | solution.py:307
  157.3 13.3 %collective-permute-start.10 = (bf16[2,256,512]{2,1,0:T(8,128)(2,1)S(1)}, bf16[2,256,512]{2,1,0:T(8,128)(2,1)S(1)}, u32[]{:S(2)}, u32[]{:S(2)}) collective-permute-start(bf16[2,256,512]{2,1,0:T(8,128)(2,1)S(1)} %add_convert_fusion.4), channel_id=1, source_target_pairs={{4,0},{8,4},{12,8},{14,12},{10,14},{6,10},{2,6},{0,2},{5,1},{9,5},... | collective-permute-start | bytes 1572872 | tf_op jit(solution)/shard_map/ppermute | solution.py:310
  158.2 13.3 %collective-permute-start.14 = (bf16[2,256,512]{2,1,0:T(8,128)(2,1)S(1)}, bf16[2,256,512]{2,1,0:T(8,128)(2,1)S(1)}, u32[]{:S(2)}, u32[]{:S(2)}) collective-permute-start(bf16[2,256,512]{2,1,0:T(8,128)(2,1)S(1)} %add_convert_fusion.2), channel_id=1, source_target_pairs={{0,4},{4,8},{8,12},{12,14},{14,10},{10,6},{6,2},{2,0},{1,5},{5,9},... | collective-permute-start | bytes 1572872 | tf_op jit(solution)/shard_map/ppermute | solution.py:307
  170.6 2.5 %copy-start.1 = (f32[2048,256]{1,0:T(8,128)S(1)}, f32[2048,256]{1,0:T(8,128)}, u32[]{:S(2)}) copy-start(f32[2048,256]{1,0:T(8,128)} %copy-done) | copy-start | bytes 6291460
  170.6 2.5 %copy-start.7 = (bf16[2,256,512]{2,1,0:T(8,128)(2,1)S(1)}, bf16[2,256,512]{2,1,0:T(8,128)(2,1)}, u32[]{:S(2)}) copy-start(bf16[2,256,512]{2,1,0:T(8,128)(2,1)} %copy-done.5) | copy-start | bytes 1572868
  170.8 9.2 %collective-permute-start.11 = (bf16[2,256,512]{2,1,0:T(8,128)(2,1)S(1)}, bf16[2,256,512]{2,1,0:T(8,128)(2,1)S(1)}, u32[]{:S(2)}, u32[]{:S(2)}) collective-permute-start(bf16[2,256,512]{2,1,0:T(8,128)(2,1)S(1)} %add_convert_fusion.3), channel_id=1, source_target_pairs={{4,0},{8,4},{12,8},{14,12},{10,14},{6,10},{2,6},{0,2},{5,1},{9,5},... | collective-permute-start | bytes 1572872 | tf_op jit(solution)/shard_map/ppermute | solution.py:310
  171.6 9.2 %collective-permute-start.15 = (bf16[2,256,512]{2,1,0:T(8,128)(2,1)S(1)}, bf16[2,256,512]{2,1,0:T(8,128)(2,1)S(1)}, u32[]{:S(2)}, u32[]{:S(2)}) collective-permute-start(bf16[2,256,512]{2,1,0:T(8,128)(2,1)S(1)} %add_convert_fusion.1), channel_id=1, source_target_pairs={{0,4},{4,8},{8,12},{12,14},{14,10},{10,6},{6,2},{2,0},{1,5},{5,9},... | collective-permute-start | bytes 1572872 | tf_op jit(solution)/shard_map/ppermute | solution.py:307
